TPU v7x, 256 devices: a whole 4x4x8 slice. The times are simulated.
256 devices in a mesh: row: 64 (over z, x, core), col: 4 (over y).
Axes of the slice: x: 4, y: 4, z: 8, core: 2. Of those that a mesh axis runs over, the one named last changes fastest.
Arguments:
- hamiltonian: bfloat16 [18432, 128, 128], P('row'), may hold values from -0.15625 to 0.15625
- block_column: int32 [18432], P('row'), may hold values from 0 to 1535, as said below
- vectors: bfloat16 [196608, 512], P('row', 'col'), may hold values from -6 to 6
Outputs:
- filtered: bfloat16 [196608, 512], P('row', 'col')
- intersection: float32 [512, 512], P('col')
Inputs may be any that keep to these rules, and one draw needn't show every extreme that they name: Block row b's entries are block_column[b * 12 + k]. Entry k = 0 is b itself. Entries k < 10 are distinct and lie among the 24 block rows of b's own index of row (block rows i * 24 to i * 24 + 23 for i = b // 24). For k >= 10, let s = (b % 24) * 2 + k - 10 and g = s // 12; the entry lies among the block rows of index (i + o) mod 64, with o = g + 1 if g < 2, else 2 - 1 - g.
All inputs are finite; a program needn't handle non-finite values.
Results may differ from a plain program's by a relative error of at most 0.0056.
Values may be sent and summed in bfloat16 or wider, within the bound.
A program may use at most 192 MiB of HBM per device.

v0:
```python
import jax
import jax.numpy as jnp
from jax import lax
from jax.sharding import PartitionSpec as P

RPR = 2
REACH = 2
STEPS = 3
filter_center = 0.2
filter_half = 0.8


def from_behind(block, axis, distance):
    devices = range(lax.axis_size(axis))
    route = [((i - distance) % len(devices), i) for i in devices]
    return lax.ppermute(block, axis, route)


def on_device(hamiltonian, block_column, vectors):
    block_size = hamiltonian.shape[1]
    row_count = vectors.shape[0] // block_size
    width_dev = vectors.shape[1]
    per_row = hamiltonian.shape[0] // row_count
    local_count = per_row - RPR
    devices = lax.axis_size("row")
    capacity = RPR * row_count // (2 * REACH)
    offsets = [number + 1 for number in range(REACH)] + [-(number + 1) for number in range(REACH)]
    matrix_rows = hamiltonian.reshape(row_count, per_row, block_size, block_size)
    columns = block_column.reshape(row_count, per_row) % row_count
    local_index = columns[:, :local_count]
    wanted = columns[:, local_count:].reshape(2 * REACH, capacity)
    spread = jnp.arange(2 * REACH * capacity) // capacity * row_count + wanted.reshape(-1)
    remote_index = spread.reshape(row_count, RPR)

    def fetch_remote(blocks):
        stacked = jnp.concatenate(
            [from_behind(blocks, "row", -offset) for offset in offsets], axis=0
        )
        return stacked[remote_index]

    def operate(blocks):
        remote = fetch_remote(blocks)
        gathered = jnp.concatenate([blocks[local_index], remote], axis=1)
        return jnp.einsum(
            "rqij,rqjk->rik", matrix_rows, gathered, preferred_element_type=jnp.float32
        )

    previous = vectors.reshape(row_count, block_size, width_dev)
    current = (
        (operate(previous) - filter_center * previous.astype(jnp.float32)) / filter_half
    ).astype(jnp.bfloat16)
    for section in range(STEPS - 1):
        product = operate(current)
        following = (
            2.0 * (product - filter_center * current.astype(jnp.float32)) / filter_half
            - previous.astype(jnp.float32)
        ).astype(jnp.bfloat16)
        previous, current = (current, following)
    filtered = current.reshape(row_count * block_size, width_dev)
    partial_value = lax.dot_general(
        filtered,
        lax.all_gather(filtered, "col", axis=1, tiled=True),
        (((0,), (0,)), ((), ())),
        preferred_element_type=jnp.float32,
    )
    summed = lax.psum(partial_value, "row")
    return (filtered, summed / (devices * row_count * block_size))


def solution(mesh):
    return jax.shard_map(
        on_device,
        mesh=mesh,
        in_specs=(P("row", None, None), P("row"), P("row", "col")),
        out_specs=(P("row", "col"), P("col", None)),
        check_vma=False,
    )
```

profile of v0, /device:TPU:1, one launch (start us, length us, event | category | flops | bytes accessed | tf_op | source)
XLA Modules:
  0.0 386.9 jit_solution(11213303579981072683)
XLA Ops:
  7.2 0.0 all-gather.2.cloned.1.call-start
  7.2 2.1 collective-permute-start.3
  9.3 2.1 collective-permute-start.2
  11.4 4.7 %collective-permute-start.1 = (bf16[24,128,128]{2,1,0:T(8,128)(2,1)}, bf16[24,128,128]{2,1,0:T(8,128)(2,1)S(1)}, u32[]{:S(2)}, u32[]{:S(2)}) collective-permute-start(bf16[24,128,128]{2,1,0:T(8,128)(2,1)} %bitcast.35), channel_id=1, source_target_pairs={{8,0},{12,4},{16,8},{20,12},{24,16},{28,20},{32,24},{36,28},{40,32... | collective-permute-start | bytes 2359304 | tf_op jit(solution)/shard_map/ppermute | solution.py:16
  16.1 1.0 collective-permute-start
  17.0 0.7 broadcast_remainder_fusion
  17.7 0.1 rem.24
  17.8 0.1 compare_select_fusion
  17.9 0.1 reshape.33
  18.0 0.1 reshape.25
  18.1 9.6 %gather_fusion = bf16[240,128,128]{2,1,0:T(8,128)(2,1)} fusion(bf16[24,128,128]{2,1,0:T(8,128)(2,1)} %bitcast.37, s32[1024]{0:T(1024)S(1)} %pad_clamp_fusion.1), kind=kCustom, calls=%fused_computation | custom fusion | bytes 15729600 | tf_op jit(solution)/shard_map/gather | solution.py:43
  27.7 5.7 %collective-permute-done.3 = bf16[24,128,128]{2,1,0:T(8,128)(2,1)S(1)} collective-permute-done((bf16[24,128,128]{2,1,0:T(8,128)(2,1)}, bf16[24,128,128]{2,1,0:T(8,128)(2,1)S(1)}, u32[]{:S(2)}, u32[]{:S(2)}) %collective-permute-start.3) | collective-permute-done | bytes 786464 | tf_op jit(solution)/shard_map/ppermute | solution.py:16
  33.4 2.1 collective-permute-done.2
  35.4 0.0 collective-permute-done.1
  35.4 3.9 %collective-permute-done = bf16[24,128,128]{2,1,0:T(8,128)(2,1)S(1)} collective-permute-done((bf16[24,128,128]{2,1,0:T(8,128)(2,1)}, bf16[24,128,128]{2,1,0:T(8,128)(2,1)S(1)}, u32[]{:S(2)}, u32[]{:S(2)}) %collective-permute-start) | collective-permute-done | bytes 786464 | tf_op jit(solution)/shard_map/ppermute | solution.py:16
  39.4 1.9 pad_maximum_fusion
  41.3 2.8 gather_fusion.1
  44.1 8.5 %fusion.14 = bf16[24,128,128]{2,1,0:T(8,128)(2,1)S(1)} fusion(bf16[24,128,128]{2,1,0:T(8,128)(2,1)S(1)} %bitcast.38, bf16[24,12,128,128]{3,2,1,0:T(8,128)(2,1)} %bitcast.49, bf16[24,2,128,128]{3,2,1,0:T(8,128)(2,1)S(1)} %bitcast.47, bf16[24,10,128,128]{3,2,1,0:T(8,128)(2,1)} %bitcast.41), kind=kOutput, calls=%fused_computation.27 | convolution fusion | flops 1228800000 | bytes 20447232 | tf_op jit(solution)/shard_map/rqij,rqjk->rik/dot_general | solution.py:44
  52.7 0.6 collective-permute-start.7
  53.2 0.2 collective-permute-start.6
  53.5 7.7 %collective-permute-start.5 = (bf16[24,128,128]{2,1,0:T(8,128)(2,1)S(1)}, bf16[24,128,128]{2,1,0:T(8,128)(2,1)}, u32[]{:S(2)}, u32[]{:S(2)}) collective-permute-start(bf16[24,128,128]{2,1,0:T(8,128)(2,1)S(1)} %fusion.14), channel_id=1, source_target_pairs={{8,0},{12,4},{16,8},{20,12},{24,16},{28,20},{32,24},{36,28},{40,32... | collective-permute-start | bytes 2359304 | tf_op jit(solution)/shard_map/ppermute | solution.py:16
  61.2 0.6 collective-permute-start.4
  61.8 8.4 %gather_fusion.2 = bf16[240,128,128]{2,1,0:T(8,128)(2,1)} fusion(bf16[24,128,128]{2,1,0:T(8,128)(2,1)S(1)} %fusion.14, s32[1024]{0:T(1024)S(1)} %pad_clamp_fusion.1), kind=kCustom, calls=%fused_computation.2 | custom fusion | bytes 15729600 | tf_op jit(solution)/shard_map/gather | solution.py:43
  70.2 7.6 %collective-permute-done.7 = bf16[24,128,128]{2,1,0:T(8,128)(2,1)S(1)} collective-permute-done((bf16[24,128,128]{2,1,0:T(8,128)(2,1)S(1)}, bf16[24,128,128]{2,1,0:T(8,128)(2,1)S(1)}, u32[]{:S(2)}, u32[]{:S(2)}) %collective-permute-start.7) | collective-permute-done | bytes 786464 | tf_op jit(solution)/shard_map/ppermute | solution.py:16
  77.8 1.2 collective-permute-done.6
  79.0 2.4 collective-permute-done.4
  81.4 3.0 pad_maximum_fusion.1
  84.5 3.9 gather_fusion.3
  88.4 9.0 %fusion.15 = bf16[24,128,128]{2,1,0:T(8,128)(2,1)S(1)} fusion(bf16[24,128,128]{2,1,0:T(8,128)(2,1)S(1)} %bitcast.39, bf16[24,128,128]{2,1,0:T(8,128)(2,1)S(1)} %fusion.14, bf16[24,12,128,128]{3,2,1,0:T(8,128)(2,1)} %bitcast.50, bf16[24,2,128,128]{3,2,1,0:T(8,128)(2,1)} %bitcast.48, bf16[24,10,128,128]{3,2,1,0:T(8,128)(2,1)} %bitcast.42), kind=kOutput, calls=%fused_computation.28 | convolution fusion | flops 1229586432 | bytes 21233664 | tf_op jit(solution)/shard_map/rqij,rqjk->rik/dot_general | solution.py:44
  97.4 3.0 collective-permute-start.11
  100.4 0.0 collective-permute-start.10
  100.4 8.1 %collective-permute-start.9 = (bf16[24,128,128]{2,1,0:T(8,128)(2,1)S(1)}, bf16[24,128,128]{2,1,0:T(8,128)(2,1)}, u32[]{:S(2)}, u32[]{:S(2)}) collective-permute-start(bf16[24,128,128]{2,1,0:T(8,128)(2,1)S(1)} %fusion.15), channel_id=1, source_target_pairs={{8,0},{12,4},{16,8},{20,12},{24,16},{28,20},{32,24},{36,28},{40,32... | collective-permute-start | bytes 2359304 | tf_op jit(solution)/shard_map/ppermute | solution.py:16
  108.5 0.7 collective-permute-start.8
  109.2 8.4 %gather_fusion.4 = bf16[240,128,128]{2,1,0:T(8,128)(2,1)} fusion(bf16[24,128,128]{2,1,0:T(8,128)(2,1)S(1)} %fusion.15, s32[1024]{0:T(1024)S(1)} %pad_clamp_fusion.1), kind=kCustom, calls=%fused_computation.4 | custom fusion | bytes 15729600 | tf_op jit(solution)/shard_map/gather | solution.py:43
  117.6 8.3 %collective-permute-done.11 = bf16[24,128,128]{2,1,0:T(8,128)(2,1)S(1)} collective-permute-done((bf16[24,128,128]{2,1,0:T(8,128)(2,1)S(1)}, bf16[24,128,128]{2,1,0:T(8,128)(2,1)S(1)}, u32[]{:S(2)}, u32[]{:S(2)}) %collective-permute-start.11) | collective-permute-done | bytes 786464 | tf_op jit(solution)/shard_map/ppermute | solution.py:16
  125.9 0.2 collective-permute-done.10
  126.2 0.0 collective-permute-done.9
  126.2 2.2 collective-permute-done.8
  128.4 3.0 pad_maximum_fusion.2
  131.4 3.9 gather_fusion.5
  135.3 9.9 %fusion.18 = bf16[24,128,128]{2,1,0:T(8,128)(2,1)} fusion(bf16[24,128,128]{2,1,0:T(8,128)(2,1)S(1)} %fusion.14, bf16[24,128,128]{2,1,0:T(8,128)(2,1)S(1)} %fusion.15, bf16[24,12,128,128]{3,2,1,0:T(8,128)(2,1)} %bitcast.51, bf16[24,2,128,128]{3,2,1,0:T(8,128)(2,1)} %bitcast.46, bf16[24,10,128,128]{3,2,1,0:T(8,128)(2,1)} %bitcast.40), kind=kOutput, calls=%fused_computation.31 | convolution fusion | flops 1229586432 | bytes 21233664 | tf_op jit(solution)/shard_map/rqij,rqjk->rik/dot_general | solution.py:44
  145.2 0.0 all-gather.2.cloned.1.call-update
  145.2 0.0 all-reduce.2.cloned.1.call-start
  145.2 52.0 %all-gather.2.cloned.1.call-done = bf16[3072,512]{1,0:T(8,128)(2,1)} async-done(((bf16[3072,128]{1,0:T(8,128)(2,1)}), bf16[3072,512]{1,0:T(8,128)(2,1)}) %all-gather.2.cloned.1.call-update) | async-done | bytes 3145744 | tf_op jit(solution)/shard_map/all_gather | solution.py:62
  197.2 3.5 fusion.32
  200.7 0.0 all-reduce.2.cloned.1.call-update
  200.7 177.7 %all-reduce.2.cloned.1.call-done = f32[128,512]{1,0:T(8,128)} async-done(((f32[128,512]{1,0:T(8,128)}), f32[128,512]{1,0:T(8,128)}) %all-reduce.2.cloned.1.call-update) | async-done | bytes 262160 | tf_op jit(solution)/shard_map/psum | solution.py:66
  378.4 1.7 broadcast_multiply_fusion
  (7 shorter events, 0.0 us)
Async XLA Ops:
  7.2 190.0 %all-gather.2.cloned.1.call-start = ((), (), s32[]{:S(2)}) async-start(), calls=%async_computation | async-start | bytes 3932160 | tf_op jit(solution)/shard_map/all_gather | solution.py:62
  7.2 26.2 %collective-permute-start.3 = (bf16[24,128,128]{2,1,0:T(8,128)(2,1)}, bf16[24,128,128]{2,1,0:T(8,128)(2,1)S(1)}, u32[]{:S(2)}, u32[]{:S(2)}) collective-permute-start(bf16[24,128,128]{2,1,0:T(8,128)(2,1)} %bitcast.33), channel_id=1, source_target_pairs={{248,0},{252,4},{0,8},{4,12},{8,16},{12,20},{16,24},{20,28},{24,32... | collective-permute-start | bytes 2359304 | tf_op jit(solution)/shard_map/ppermute | solution.py:16
  9.3 26.1 %collective-permute-start.2 = (bf16[24,128,128]{2,1,0:T(8,128)(2,1)}, bf16[24,128,128]{2,1,0:T(8,128)(2,1)S(1)}, u32[]{:S(2)}, u32[]{:S(2)}) collective-permute-start(bf16[24,128,128]{2,1,0:T(8,128)(2,1)} %bitcast.34), channel_id=1, source_target_pairs={{252,0},{0,4},{4,8},{8,12},{12,16},{16,20},{20,24},{24,28},{28,32}... | collective-permute-start | bytes 2359304 | tf_op jit(solution)/shard_map/ppermute | solution.py:16
  11.4 24.1 %collective-permute-start.1 = (bf16[24,128,128]{2,1,0:T(8,128)(2,1)}, bf16[24,128,128]{2,1,0:T(8,128)(2,1)S(1)}, u32[]{:S(2)}, u32[]{:S(2)}) collective-permute-start(bf16[24,128,128]{2,1,0:T(8,128)(2,1)} %bitcast.35), channel_id=1, source_target_pairs={{8,0},{12,4},{16,8},{20,12},{24,16},{28,20},{32,24},{36,28},{40,32... | collective-permute-start | bytes 2359304 | tf_op jit(solution)/shard_map/ppermute | solution.py:16
  16.1 23.3 %collective-permute-start = (bf16[24,128,128]{2,1,0:T(8,128)(2,1)}, bf16[24,128,128]{2,1,0:T(8,128)(2,1)S(1)}, u32[]{:S(2)}, u32[]{:S(2)}) collective-permute-start(bf16[24,128,128]{2,1,0:T(8,128)(2,1)} %bitcast.36), channel_id=1, source_target_pairs={{4,0},{8,4},{12,8},{16,12},{20,16},{24,20},{28,24},{32,28},{36,32}... | collective-permute-start | bytes 2359304 | tf_op jit(solution)/shard_map/ppermute | solution.py:16
  41.3 2.8 copy-start
  52.7 25.1 %collective-permute-start.7 = (bf16[24,128,128]{2,1,0:T(8,128)(2,1)S(1)}, bf16[24,128,128]{2,1,0:T(8,128)(2,1)S(1)}, u32[]{:S(2)}, u32[]{:S(2)}) collective-permute-start(bf16[24,128,128]{2,1,0:T(8,128)(2,1)S(1)} %fusion.14), channel_id=1, source_target_pairs={{248,0},{252,4},{0,8},{4,12},{8,16},{12,20},{16,24},{20,28},{24,32... | collective-permute-start | bytes 2359304 | tf_op jit(solution)/shard_map/ppermute | solution.py:16
  53.2 25.8 %collective-permute-start.6 = (bf16[24,128,128]{2,1,0:T(8,128)(2,1)S(1)}, bf16[24,128,128]{2,1,0:T(8,128)(2,1)S(1)}, u32[]{:S(2)}, u32[]{:S(2)}) collective-permute-start(bf16[24,128,128]{2,1,0:T(8,128)(2,1)S(1)} %fusion.14), channel_id=1, source_target_pairs={{252,0},{0,4},{4,8},{8,12},{12,16},{16,20},{20,24},{24,28},{28,32}... | collective-permute-start | bytes 2359304 | tf_op jit(solution)/shard_map/ppermute | solution.py:16
  53.5 25.6 %collective-permute-start.5 = (bf16[24,128,128]{2,1,0:T(8,128)(2,1)S(1)}, bf16[24,128,128]{2,1,0:T(8,128)(2,1)}, u32[]{:S(2)}, u32[]{:S(2)}) collective-permute-start(bf16[24,128,128]{2,1,0:T(8,128)(2,1)S(1)} %fusion.14), channel_id=1, source_target_pairs={{8,0},{12,4},{16,8},{20,12},{24,16},{28,20},{32,24},{36,28},{40,32... | collective-permute-start | bytes 2359304 | tf_op jit(solution)/shard_map/ppermute | solution.py:16
  61.2 20.3 %collective-permute-start.4 = (bf16[24,128,128]{2,1,0:T(8,128)(2,1)S(1)}, bf16[24,128,128]{2,1,0:T(8,128)(2,1)}, u32[]{:S(2)}, u32[]{:S(2)}) collective-permute-start(bf16[24,128,128]{2,1,0:T(8,128)(2,1)S(1)} %fusion.14), channel_id=1, source_target_pairs={{4,0},{8,4},{12,8},{16,12},{20,16},{24,20},{28,24},{32,28},{36,32}... | collective-permute-start | bytes 2359304 | tf_op jit(solution)/shard_map/ppermute | solution.py:16
  97.4 28.5 %collective-permute-start.11 = (bf16[24,128,128]{2,1,0:T(8,128)(2,1)S(1)}, bf16[24,128,128]{2,1,0:T(8,128)(2,1)S(1)}, u32[]{:S(2)}, u32[]{:S(2)}) collective-permute-start(bf16[24,128,128]{2,1,0:T(8,128)(2,1)S(1)} %fusion.15), channel_id=1, source_target_pairs={{248,0},{252,4},{0,8},{4,12},{8,16},{12,20},{16,24},{20,28},{24,32... | collective-permute-start | bytes 2359304 | tf_op jit(solution)/shard_map/ppermute | solution.py:16
  100.4 25.8 %collective-permute-start.10 = (bf16[24,128,128]{2,1,0:T(8,128)(2,1)S(1)}, bf16[24,128,128]{2,1,0:T(8,128)(2,1)S(1)}, u32[]{:S(2)}, u32[]{:S(2)}) collective-permute-start(bf16[24,128,128]{2,1,0:T(8,128)(2,1)S(1)} %fusion.15), channel_id=1, source_target_pairs={{252,0},{0,4},{4,8},{8,12},{12,16},{16,20},{20,24},{24,28},{28,32}... | collective-permute-start | bytes 2359304 | tf_op jit(solution)/shard_map/ppermute | solution.py:16
  100.4 25.8 %collective-permute-start.9 = (bf16[24,128,128]{2,1,0:T(8,128)(2,1)S(1)}, bf16[24,128,128]{2,1,0:T(8,128)(2,1)}, u32[]{:S(2)}, u32[]{:S(2)}) collective-permute-start(bf16[24,128,128]{2,1,0:T(8,128)(2,1)S(1)} %fusion.15), channel_id=1, source_target_pairs={{8,0},{12,4},{16,8},{20,12},{24,16},{28,20},{32,24},{36,28},{40,32... | collective-permute-start | bytes 2359304 | tf_op jit(solution)/shard_map/ppermute | solution.py:16
  108.5 19.9 %collective-permute-start.8 = (bf16[24,128,128]{2,1,0:T(8,128)(2,1)S(1)}, bf16[24,128,128]{2,1,0:T(8,128)(2,1)}, u32[]{:S(2)}, u32[]{:S(2)}) collective-permute-start(bf16[24,128,128]{2,1,0:T(8,128)(2,1)S(1)} %fusion.15), channel_id=1, source_target_pairs={{4,0},{8,4},{12,8},{16,12},{20,16},{24,20},{28,24},{32,28},{36,32}... | collective-permute-start | bytes 2359304 | tf_op jit(solution)/shard_map/ppermute | solution.py:16
  145.2 233.2 %all-reduce.2.cloned.1.call-start = ((), (), s32[]{:S(2)}) async-start(), calls=%async_computation.1 | async-start | bytes 524288 | tf_op jit(solution)/shard_map/psum | solution.py:66
Sparse Core Ops, SparseCore 0:
  145.3 51.8 all-gather.1
  201.3 177.0 all-reduce.1
where the time goes:
time: 387 us
  waiting for transfers between devices  263 us (68%)
  local copies, waits for them, and re-layouts  37.2 us (10%)
  matrix products  30.9 us (8%)
  starting transfers between devices  30.8 us (8%)
  between operations  14.1 us (4%)
  other arithmetic  10.5 us (3%)
    psum x1, waiting for transfers between devices, on_device(): summed = lax.psum(partial_value, 'row')  178 us
    all_gather x1, waiting for transfers between devices, on_device(): lax.all_gather(filtered, 'col', axis=1, tiled=True)  52 us
    ppermute x12, waiting for transfers between devices, from_behind(): return lax.ppermute(block, axis, route)  33.7 us
    ppermute x12, starting transfers between devices, from_behind(): return lax.ppermute(block, axis, route)  30.7 us
    dot_general x3, matrix products, operate(): jnp.einsum('rqij,rqjk->rik', matrix_rows, gathered, preferred_element_typ...  27.4 us
    gather x3, local copies, waits for them, and re-layouts, operate(): gathered = jnp.concatenate([blocks[local_index], remote], axis=1)  26.4 us
    gather x3, local copies, waits for them, and re-layouts, fetch_remote(): return stacked[remote_index]  10.5 us
    concatenate x3, other arithmetic, fetch_remote(): jnp.concatenate([from_behind(blocks, 'row', -offset) for offset in offset...  8.01 us
  transfers between devices with their start and end apart: 14, of which 11 were waited for; matrix products, arithmetic and copies ran while one was open for 7% of the time, Pallas kernels for 0%

commit v1 on v0

--- a/solution.py
+++ b/solution.py
@@ -59,7 +59,9 @@
     filtered = current.reshape(row_count * block_size, width_dev)
     partial_value = lax.dot_general(
         filtered,
-        lax.all_gather(filtered, "col", axis=1, tiled=True),
+        jnp.concatenate(
+            lax.all_to_all(jnp.stack([filtered] * lax.axis_size("col")), "col", 0, 0), axis=1
+        ),
         (((0,), (0,)), ((), ())),
         preferred_element_type=jnp.float32,
     )

time: 387 us -> 376 us (0.972)
  waiting for transfers between devices: 263 us -> 219 us
  blocking collectives: 0 us -> 34.3 us
    all_gather x1 -> x0, waiting for transfers between devices: 52 us -> none  [on_device(): lax.all_gather(filtered, 'col', axis=1, tiled=True)]
    all_to_all x0 -> x1, blocking collectives: none -> 34.3 us  [on_device(): lax.all_to_all(jnp.stack([filtered] * lax.axis_size('col')), 'col', 0, 0)]
    psum x1, waiting for transfers between devices: 178 us -> 185 us  [on_device(): summed = lax.psum(partial_value, 'row')]
  transfers between devices with their start and end apart: 14 -> 13, of which waited for: 11 -> 10; matrix products, arithmetic and copies ran while one was open for 7% -> 7% of each run, Pallas kernels for 0% -> 0%
where the time goes in v1:
time: 376 us; the launch traced here: 375 us
  waiting for transfers between devices  219 us (58%)
  local copies, waits for them, and re-layouts  37.9 us (10%)
  blocking collectives  34.3 us (9%)
  starting transfers between devices  30.8 us (8%)
  matrix products  28.4 us (8%)
  between operations  14.1 us (4%)
  other arithmetic  10.5 us (3%)
    psum x1, waiting for transfers between devices, on_device(): summed = lax.psum(partial_value, 'row')  185 us
    all_to_all x1, blocking collectives, on_device(): lax.all_to_all(jnp.stack([filtered] * lax.axis_size('col')), 'col', 0, 0)  34.3 us
    ppermute x12, waiting for transfers between devices, from_behind(): return lax.ppermute(block, axis, route)  33.7 us
    ppermute x12, starting transfers between devices, from_behind(): return lax.ppermute(block, axis, route)  30.7 us
    dot_general x3, matrix products, operate(): jnp.einsum('rqij,rqjk->rik', matrix_rows, gathered, preferred_element_typ...  26.5 us
    gather x3, local copies, waits for them, and re-layouts, operate(): gathered = jnp.concatenate([blocks[local_index], remote], axis=1)  26.4 us
    gather x3, local copies, waits for them, and re-layouts, fetch_remote(): return stacked[remote_index]  10.5 us
    concatenate x3, other arithmetic, fetch_remote(): jnp.concatenate([from_behind(blocks, 'row', -offset) for offset in offset...  8.06 us
  transfers between devices with their start and end apart: 13, of which 10 were waited for; matrix products, arithmetic and copies ran while one was open for 7% of the time, Pallas kernels for 0%

profile of v1, /device:TPU:1, one launch (start us, length us, event | category | flops | bytes accessed | tf_op | source)
XLA Modules:
  0.0 375.2 jit_solution(15338089175555413936)
XLA Ops:
  7.2 0.0 all-reduce.2.cloned.1.call-start
  7.2 2.1 collective-permute-start.3
  9.3 2.1 collective-permute-start.2
  11.4 4.7 %collective-permute-start.1 = (bf16[24,128,128]{2,1,0:T(8,128)(2,1)}, bf16[24,128,128]{2,1,0:T(8,128)(2,1)S(1)}, u32[]{:S(2)}, u32[]{:S(2)}) collective-permute-start(bf16[24,128,128]{2,1,0:T(8,128)(2,1)} %bitcast.38), channel_id=1, source_target_pairs={{8,0},{12,4},{16,8},{20,12},{24,16},{28,20},{32,24},{36,28},{40,32... | collective-permute-start | bytes 2359304 | tf_op jit(solution)/shard_map/ppermute | solution.py:16
  16.1 1.0 collective-permute-start
  17.0 0.7 broadcast_remainder_fusion
  17.7 0.1 rem.24
  17.8 0.1 compare_select_fusion
  17.9 0.1 reshape.43
  18.0 0.1 reshape.35
  18.1 9.6 %gather_fusion = bf16[240,128,128]{2,1,0:T(8,128)(2,1)} fusion(bf16[24,128,128]{2,1,0:T(8,128)(2,1)} %bitcast.40, s32[1024]{0:T(1024)S(1)} %pad_clamp_fusion.1), kind=kCustom, calls=%fused_computation | custom fusion | bytes 15729600 | tf_op jit(solution)/shard_map/gather | solution.py:43
  27.7 5.7 %collective-permute-done.3 = bf16[24,128,128]{2,1,0:T(8,128)(2,1)S(1)} collective-permute-done((bf16[24,128,128]{2,1,0:T(8,128)(2,1)}, bf16[24,128,128]{2,1,0:T(8,128)(2,1)S(1)}, u32[]{:S(2)}, u32[]{:S(2)}) %collective-permute-start.3) | collective-permute-done | bytes 786464 | tf_op jit(solution)/shard_map/ppermute | solution.py:16
  33.4 2.1 collective-permute-done.2
  35.4 3.9 %collective-permute-done = bf16[24,128,128]{2,1,0:T(8,128)(2,1)S(1)} collective-permute-done((bf16[24,128,128]{2,1,0:T(8,128)(2,1)}, bf16[24,128,128]{2,1,0:T(8,128)(2,1)S(1)}, u32[]{:S(2)}, u32[]{:S(2)}) %collective-permute-start) | collective-permute-done | bytes 786464 | tf_op jit(solution)/shard_map/ppermute | solution.py:16
  39.4 1.9 pad_maximum_fusion
  41.3 2.8 gather_fusion.1
  44.1 8.5 %fusion.14 = bf16[24,128,128]{2,1,0:T(8,128)(2,1)S(1)} fusion(bf16[24,128,128]{2,1,0:T(8,128)(2,1)S(1)} %bitcast.41, bf16[24,12,128,128]{3,2,1,0:T(8,128)(2,1)} %bitcast.53, bf16[24,2,128,128]{3,2,1,0:T(8,128)(2,1)S(1)} %bitcast.51, bf16[24,10,128,128]{3,2,1,0:T(8,128)(2,1)} %bitcast.45), kind=kOutput, calls=%fused_computation.27 | convolution fusion | flops 1228800000 | bytes 20447232 | tf_op jit(solution)/shard_map/rqij,rqjk->rik/dot_general | solution.py:44
  52.7 0.6 collective-permute-start.7
  53.2 0.2 collective-permute-start.6
  53.5 7.7 %collective-permute-start.5 = (bf16[24,128,128]{2,1,0:T(8,128)(2,1)S(1)}, bf16[24,128,128]{2,1,0:T(8,128)(2,1)}, u32[]{:S(2)}, u32[]{:S(2)}) collective-permute-start(bf16[24,128,128]{2,1,0:T(8,128)(2,1)S(1)} %fusion.14), channel_id=1, source_target_pairs={{8,0},{12,4},{16,8},{20,12},{24,16},{28,20},{32,24},{36,28},{40,32... | collective-permute-start | bytes 2359304 | tf_op jit(solution)/shard_map/ppermute | solution.py:16
  61.2 0.6 collective-permute-start.4
  61.8 8.4 %gather_fusion.2 = bf16[240,128,128]{2,1,0:T(8,128)(2,1)} fusion(bf16[24,128,128]{2,1,0:T(8,128)(2,1)S(1)} %fusion.14, s32[1024]{0:T(1024)S(1)} %pad_clamp_fusion.1), kind=kCustom, calls=%fused_computation.2 | custom fusion | bytes 15729600 | tf_op jit(solution)/shard_map/gather | solution.py:43
  70.2 7.6 %collective-permute-done.7 = bf16[24,128,128]{2,1,0:T(8,128)(2,1)S(1)} collective-permute-done((bf16[24,128,128]{2,1,0:T(8,128)(2,1)S(1)}, bf16[24,128,128]{2,1,0:T(8,128)(2,1)S(1)}, u32[]{:S(2)}, u32[]{:S(2)}) %collective-permute-start.7) | collective-permute-done | bytes 786464 | tf_op jit(solution)/shard_map/ppermute | solution.py:16
  77.8 1.2 collective-permute-done.6
  79.0 0.0 collective-permute-done.5
  79.0 2.4 collective-permute-done.4
  81.5 3.1 pad_maximum_fusion.1
  84.5 3.9 %gather_fusion.3 = bf16[48,128,128]{2,1,0:T(8,128)(2,1)} fusion(bf16[96,128,128]{2,1,0:T(8,128)(2,1)} %pad_maximum_fusion.1, s32[1024]{0:T(1024)S(1)} %pad_clamp_fusion), kind=kCustom, calls=%fused_computation.3 | custom fusion | bytes 3145920 | tf_op jit(solution)/shard_map/gather | solution.py:39
  88.4 9.0 %fusion.15 = bf16[24,128,128]{2,1,0:T(8,128)(2,1)S(1)} fusion(bf16[24,128,128]{2,1,0:T(8,128)(2,1)S(1)} %bitcast.42, bf16[24,128,128]{2,1,0:T(8,128)(2,1)S(1)} %fusion.14, bf16[24,12,128,128]{3,2,1,0:T(8,128)(2,1)} %bitcast.54, bf16[24,2,128,128]{3,2,1,0:T(8,128)(2,1)} %bitcast.52, bf16[24,10,128,128]{3,2,1,0:T(8,128)(2,1)} %bitcast.46), kind=kOutput, calls=%fused_computation.28 | convolution fusion | flops 1229586432 | bytes 21233664 | tf_op jit(solution)/shard_map/rqij,rqjk->rik/dot_general | solution.py:44
  97.4 3.0 collective-permute-start.11
  100.4 0.0 collective-permute-start.10
  100.4 8.1 %collective-permute-start.9 = (bf16[24,128,128]{2,1,0:T(8,128)(2,1)S(1)}, bf16[24,128,128]{2,1,0:T(8,128)(2,1)}, u32[]{:S(2)}, u32[]{:S(2)}) collective-permute-start(bf16[24,128,128]{2,1,0:T(8,128)(2,1)S(1)} %fusion.15), channel_id=1, source_target_pairs={{8,0},{12,4},{16,8},{20,12},{24,16},{28,20},{32,24},{36,28},{40,32... | collective-permute-start | bytes 2359304 | tf_op jit(solution)/shard_map/ppermute | solution.py:16
  108.5 0.7 collective-permute-start.8
  109.2 8.4 %gather_fusion.4 = bf16[240,128,128]{2,1,0:T(8,128)(2,1)} fusion(bf16[24,128,128]{2,1,0:T(8,128)(2,1)S(1)} %fusion.15, s32[1024]{0:T(1024)S(1)} %pad_clamp_fusion.1), kind=kCustom, calls=%fused_computation.4 | custom fusion | bytes 15729600 | tf_op jit(solution)/shard_map/gather | solution.py:43
  117.6 8.3 %collective-permute-done.11 = bf16[24,128,128]{2,1,0:T(8,128)(2,1)S(1)} collective-permute-done((bf16[24,128,128]{2,1,0:T(8,128)(2,1)S(1)}, bf16[24,128,128]{2,1,0:T(8,128)(2,1)S(1)}, u32[]{:S(2)}, u32[]{:S(2)}) %collective-permute-start.11) | collective-permute-done | bytes 786464 | tf_op jit(solution)/shard_map/ppermute | solution.py:16
  125.9 0.2 collective-permute-done.10
  126.2 2.2 collective-permute-done.8
  128.4 3.1 pad_maximum_fusion.2
  131.5 3.9 %gather_fusion.5 = bf16[48,128,128]{2,1,0:T(8,128)(2,1)} fusion(bf16[96,128,128]{2,1,0:T(8,128)(2,1)} %pad_maximum_fusion.2, s32[1024]{0:T(1024)S(1)} %pad_clamp_fusion), kind=kCustom, calls=%fused_computation.5 | custom fusion | bytes 3145920 | tf_op jit(solution)/shard_map/gather | solution.py:39
  135.3 9.0 %fusion.18 = bf16[24,128,128]{2,1,0:T(8,128)(2,1)S(1)} fusion(bf16[24,128,128]{2,1,0:T(8,128)(2,1)S(1)} %fusion.14, bf16[24,128,128]{2,1,0:T(8,128)(2,1)S(1)} %fusion.15, bf16[24,12,128,128]{3,2,1,0:T(8,128)(2,1)} %bitcast.55, bf16[24,2,128,128]{3,2,1,0:T(8,128)(2,1)} %bitcast.50, bf16[24,10,128,128]{3,2,1,0:T(8,128)(2,1)} %bitcast.44), kind=kOutput, calls=%fused_computation.31 | convolution fusion | flops 1229586432 | bytes 21233664 | tf_op jit(solution)/shard_map/rqij,rqjk->rik/dot_general | solution.py:44
  144.3 0.0 copy-start.1
  144.3 0.3 copy.5
  144.6 0.4 stack.3
  145.0 34.3 %all_to_all.5 = bf16[4,3072,128]{1,2,0:T(8,128)(2,1)S(1)} all-to-all(bf16[4,3072,128]{1,2,0:T(8,128)(2,1)S(1)} %stack.3), channel_id=1, replica_groups=mesh['row'=64,'col'=4] {'col'}, dimensions={0} | all-to-all | bytes 6291456 | tf_op jit(solution)/shard_map/all_to_all | solution.py:63
  179.3 1.9 fusion.32
  181.2 0.0 all-reduce.2.cloned.1.call-update
  181.2 185.5 %all-reduce.2.cloned.1.call-done = f32[128,512]{1,0:T(8,128)} async-done(((f32[128,512]{1,0:T(8,128)}), f32[128,512]{1,0:T(8,128)}) %all-reduce.2.cloned.1.call-update) | async-done | bytes 262160 | tf_op jit(solution)/shard_map/psum | solution.py:68
  366.7 1.7 broadcast_multiply_fusion
  (9 shorter events, 0.0 us)
Async XLA Ops:
  7.2 359.6 %all-reduce.2.cloned.1.call-start = ((), (), s32[]{:S(2)}) async-start(), calls=%async_computation.1 | async-start | bytes 524288 | tf_op jit(solution)/shard_map/psum | solution.py:68
  7.2 26.2 %collective-permute-start.3 = (bf16[24,128,128]{2,1,0:T(8,128)(2,1)}, bf16[24,128,128]{2,1,0:T(8,128)(2,1)S(1)}, u32[]{:S(2)}, u32[]{:S(2)}) collective-permute-start(bf16[24,128,128]{2,1,0:T(8,128)(2,1)} %bitcast.36), channel_id=1, source_target_pairs={{248,0},{252,4},{0,8},{4,12},{8,16},{12,20},{16,24},{20,28},{24,32... | collective-permute-start | bytes 2359304 | tf_op jit(solution)/shard_map/ppermute | solution.py:16
  9.3 26.1 %collective-permute-start.2 = (bf16[24,128,128]{2,1,0:T(8,128)(2,1)}, bf16[24,128,128]{2,1,0:T(8,128)(2,1)S(1)}, u32[]{:S(2)}, u32[]{:S(2)}) collective-permute-start(bf16[24,128,128]{2,1,0:T(8,128)(2,1)} %bitcast.37), channel_id=1, source_target_pairs={{252,0},{0,4},{4,8},{8,12},{12,16},{16,20},{20,24},{24,28},{28,32}... | collective-permute-start | bytes 2359304 | tf_op jit(solution)/shard_map/ppermute | solution.py:16
  11.4 24.1 %collective-permute-start.1 = (bf16[24,128,128]{2,1,0:T(8,128)(2,1)}, bf16[24,128,128]{2,1,0:T(8,128)(2,1)S(1)}, u32[]{:S(2)}, u32[]{:S(2)}) collective-permute-start(bf16[24,128,128]{2,1,0:T(8,128)(2,1)} %bitcast.38), channel_id=1, source_target_pairs={{8,0},{12,4},{16,8},{20,12},{24,16},{28,20},{32,24},{36,28},{40,32... | collective-permute-start | bytes 2359304 | tf_op jit(solution)/shard_map/ppermute | solution.py:16
  16.1 23.3 %collective-permute-start = (bf16[24,128,128]{2,1,0:T(8,128)(2,1)}, bf16[24,128,128]{2,1,0:T(8,128)(2,1)S(1)}, u32[]{:S(2)}, u32[]{:S(2)}) collective-permute-start(bf16[24,128,128]{2,1,0:T(8,128)(2,1)} %bitcast.39), channel_id=1, source_target_pairs={{4,0},{8,4},{12,8},{16,12},{20,16},{24,20},{28,24},{32,28},{36,32}... | collective-permute-start | bytes 2359304 | tf_op jit(solution)/shard_map/ppermute | solution.py:16
  41.3 2.8 copy-start
  52.7 25.1 %collective-permute-start.7 = (bf16[24,128,128]{2,1,0:T(8,128)(2,1)S(1)}, bf16[24,128,128]{2,1,0:T(8,128)(2,1)S(1)}, u32[]{:S(2)}, u32[]{:S(2)}) collective-permute-start(bf16[24,128,128]{2,1,0:T(8,128)(2,1)S(1)} %fusion.14), channel_id=1, source_target_pairs={{248,0},{252,4},{0,8},{4,12},{8,16},{12,20},{16,24},{20,28},{24,32... | collective-permute-start | bytes 2359304 | tf_op jit(solution)/shard_map/ppermute | solution.py:16
  53.2 25.8 %collective-permute-start.6 = (bf16[24,128,128]{2,1,0:T(8,128)(2,1)S(1)}, bf16[24,128,128]{2,1,0:T(8,128)(2,1)S(1)}, u32[]{:S(2)}, u32[]{:S(2)}) collective-permute-start(bf16[24,128,128]{2,1,0:T(8,128)(2,1)S(1)} %fusion.14), channel_id=1, source_target_pairs={{252,0},{0,4},{4,8},{8,12},{12,16},{16,20},{20,24},{24,28},{28,32}... | collective-permute-start | bytes 2359304 | tf_op jit(solution)/shard_map/ppermute | solution.py:16
  53.5 25.6 %collective-permute-start.5 = (bf16[24,128,128]{2,1,0:T(8,128)(2,1)S(1)}, bf16[24,128,128]{2,1,0:T(8,128)(2,1)}, u32[]{:S(2)}, u32[]{:S(2)}) collective-permute-start(bf16[24,128,128]{2,1,0:T(8,128)(2,1)S(1)} %fusion.14), channel_id=1, source_target_pairs={{8,0},{12,4},{16,8},{20,12},{24,16},{28,20},{32,24},{36,28},{40,32... | collective-permute-start | bytes 2359304 | tf_op jit(solution)/shard_map/ppermute | solution.py:16
  61.2 20.3 %collective-permute-start.4 = (bf16[24,128,128]{2,1,0:T(8,128)(2,1)S(1)}, bf16[24,128,128]{2,1,0:T(8,128)(2,1)}, u32[]{:S(2)}, u32[]{:S(2)}) collective-permute-start(bf16[24,128,128]{2,1,0:T(8,128)(2,1)S(1)} %fusion.14), channel_id=1, source_target_pairs={{4,0},{8,4},{12,8},{16,12},{20,16},{24,20},{28,24},{32,28},{36,32}... | collective-permute-start | bytes 2359304 | tf_op jit(solution)/shard_map/ppermute | solution.py:16
  97.4 28.5 %collective-permute-start.11 = (bf16[24,128,128]{2,1,0:T(8,128)(2,1)S(1)}, bf16[24,128,128]{2,1,0:T(8,128)(2,1)S(1)}, u32[]{:S(2)}, u32[]{:S(2)}) collective-permute-start(bf16[24,128,128]{2,1,0:T(8,128)(2,1)S(1)} %fusion.15), channel_id=1, source_target_pairs={{248,0},{252,4},{0,8},{4,12},{8,16},{12,20},{16,24},{20,28},{24,32... | collective-permute-start | bytes 2359304 | tf_op jit(solution)/shard_map/ppermute | solution.py:16
  100.4 25.8 %collective-permute-start.10 = (bf16[24,128,128]{2,1,0:T(8,128)(2,1)S(1)}, bf16[24,128,128]{2,1,0:T(8,128)(2,1)S(1)}, u32[]{:S(2)}, u32[]{:S(2)}) collective-permute-start(bf16[24,128,128]{2,1,0:T(8,128)(2,1)S(1)} %fusion.15), channel_id=1, source_target_pairs={{252,0},{0,4},{4,8},{8,12},{12,16},{16,20},{20,24},{24,28},{28,32}... | collective-permute-start | bytes 2359304 | tf_op jit(solution)/shard_map/ppermute | solution.py:16
  100.4 25.8 %collective-permute-start.9 = (bf16[24,128,128]{2,1,0:T(8,128)(2,1)S(1)}, bf16[24,128,128]{2,1,0:T(8,128)(2,1)}, u32[]{:S(2)}, u32[]{:S(2)}) collective-permute-start(bf16[24,128,128]{2,1,0:T(8,128)(2,1)S(1)} %fusion.15), channel_id=1, source_target_pairs={{8,0},{12,4},{16,8},{20,12},{24,16},{28,20},{32,24},{36,28},{40,32... | collective-permute-start | bytes 2359304 | tf_op jit(solution)/shard_map/ppermute | solution.py:16
  108.5 19.9 %collective-permute-start.8 = (bf16[24,128,128]{2,1,0:T(8,128)(2,1)S(1)}, bf16[24,128,128]{2,1,0:T(8,128)(2,1)}, u32[]{:S(2)}, u32[]{:S(2)}) collective-permute-start(bf16[24,128,128]{2,1,0:T(8,128)(2,1)S(1)} %fusion.15), channel_id=1, source_target_pairs={{4,0},{8,4},{12,8},{16,12},{20,16},{24,20},{28,24},{32,28},{36,32}... | collective-permute-start | bytes 2359304 | tf_op jit(solution)/shard_map/ppermute | solution.py:16
  144.3 35.0 %copy-start.1 = (bf16[24,128,128]{2,1,0:T(8,128)(2,1)}, bf16[24,128,128]{2,1,0:T(8,128)(2,1)S(1)}, u32[]{:S(2)}) copy-start(bf16[24,128,128]{2,1,0:T(8,128)(2,1)S(1)} %fusion.18) | copy-start | bytes 2359300
Sparse Core Ops, SparseCore 0:
  181.3 185.3 all-reduce.1
